TPU v7x, 128 devices: a whole 4x4x4 slice. The times are simulated.
128 devices in a mesh: seq: 32 (over y, x_hi, z), dp: 4 (over x_lo, core).
Axes of the slice: x: 4 (x_hi: 2, x_lo: 2; x = x_hi * 2 + x_lo), y: 4, z: 4, core: 2. Of those that a mesh axis runs over, the one named last changes fastest.
Arguments:
- spectra_in: bfloat16 [24, 2048, 768], P('dp', 'seq'), may hold values from -6 to 6
- cotangent: bfloat16 [24, 2048, 768], P('dp', 'seq'), may hold values from -6 to 6
- tok_in_w: bfloat16 [2048, 1024], P('seq'), may hold values from -0.125 to 0.125
- tok_out_w: bfloat16 [2048, 1024], P('seq'), may hold values from -0.1875 to 0.1875
- ch_in_w: bfloat16 [1536, 768], replicated, may hold values from -0.21875 to 0.21875
- ch_out_w: bfloat16 [1536, 768], replicated, may hold values from -0.15625 to 0.15625
Outputs:
- grad_input: bfloat16 [24, 2048, 768], P('dp', 'seq')
- grad_tok_in: float32 [2048, 1024], P(('seq', 'dp'))
- grad_tok_out: float32 [2048, 1024], P(('seq', 'dp'))
- grad_ch_in: float32 [1536, 768], P(('seq', 'dp'))
- grad_ch_out: float32 [1536, 768], P(('seq', 'dp'))
All inputs are finite; a program needn't handle non-finite values.
Results may differ from a plain program's by a relative error of at most 0.012.
Values may be sent and summed in bfloat16 or wider, within the bound.
A program may use at most 192 MiB of HBM per device.

v0:
```python
import math

import jax
import jax.numpy as jnp
from jax import lax
from jax.sharding import PartitionSpec as P


def normalize(values):
    center = values - jnp.mean(values, axis=-1, keepdims=True)
    inv_scale = lax.rsqrt(jnp.mean(center * center, axis=-1, keepdims=True) + 1e-05)
    return (center * inv_scale, inv_scale)


def norm_back(unit, inv_scale, upstream):
    first = jnp.mean(upstream, axis=-1, keepdims=True)
    second = jnp.mean(upstream * unit, axis=-1, keepdims=True)
    return inv_scale * (upstream - first - unit * second)


def gelu_pair(values):
    factor = math.sqrt(2.0 / math.pi)
    inner = factor * (values + 0.044715 * values * values * values)
    tangent = jnp.tanh(inner)
    result = 0.5 * values * (1.0 + tangent)
    slope = 0.5 * (1.0 + tangent) + 0.5 * values * (1.0 - tangent * tangent) * factor * (
        1.0 + 3.0 * 0.044715 * values * values
    )
    return (result, slope)


def to_channels(patch_major):
    flipped = jnp.swapaxes(patch_major, 1, 2)
    return lax.all_to_all(flipped, "seq", split_axis=1, concat_axis=2, tiled=True)


def to_patches(channel_major):
    moved = lax.all_to_all(channel_major, "seq", split_axis=2, concat_axis=1, tiled=True)
    return jnp.swapaxes(moved, 1, 2)


def local(spectra_in, cotangent, tok_in_w, tok_out_w, ch_in_w, ch_out_w):
    whole_in, whole_out = (
        lax.all_gather(tok_in_w, "seq", axis=0, tiled=True),
        lax.all_gather(tok_out_w, "seq", axis=0, tiled=True),
    )
    width_hid = tok_in_w.shape[1]
    width_chan = spectra_in.shape[2]
    source = spectra_in.astype(jnp.float32)
    unit_first, scale_first = normalize(source)
    normed = unit_first.astype(jnp.bfloat16)
    normed_cols = to_channels(normed)
    hidden = jnp.einsum("scp,pj->scj", normed_cols, whole_in, preferred_element_type=jnp.float32)
    hidden_val, hidden_slope = gelu_pair(hidden)
    token_act = hidden_val.astype(jnp.bfloat16)
    mix_cols = jnp.einsum(
        "scj,pj->scp", token_act, whole_out, preferred_element_type=jnp.float32
    ).astype(jnp.bfloat16)
    token_mix = to_patches(mix_cols)
    middle = (source + token_mix.astype(jnp.float32)).astype(jnp.bfloat16)
    unit_second, scale_second = normalize(middle.astype(jnp.float32))
    normed_second = unit_second.astype(jnp.bfloat16)
    chan_pre = jnp.einsum("spc,hc->sph", normed_second, ch_in_w, preferred_element_type=jnp.float32)
    chan_val, chan_slope = gelu_pair(chan_pre)
    chan_act = chan_val.astype(jnp.bfloat16)
    chan_down = jnp.einsum("spc,hc->sph", cotangent, ch_out_w, preferred_element_type=jnp.float32)
    chan_grad = (chan_down * chan_slope).astype(jnp.bfloat16)
    grad_up = jnp.einsum(
        "sph,spc->hc", chan_grad, normed_second, preferred_element_type=jnp.float32
    )
    grad_down = jnp.einsum("sph,spc->hc", chan_act, cotangent, preferred_element_type=jnp.float32)
    chan_sums = lax.psum_scatter(
        jnp.concatenate([grad_up, grad_down], axis=1),
        ("seq", "dp"),
        scatter_dimension=0,
        tiled=True,
    )
    grad_ch_in = chan_sums[:, :width_chan]
    grad_ch_out = chan_sums[:, width_chan:]
    second_up = jnp.einsum("sph,hc->spc", chan_grad, ch_in_w, preferred_element_type=jnp.float32)
    middle_grad = cotangent.astype(jnp.float32) + norm_back(unit_second, scale_second, second_up)
    mix_grad = middle_grad.astype(jnp.bfloat16)
    mix_cols_grad = to_channels(mix_grad)
    hidden_up = jnp.einsum(
        "scp,pj->scj", mix_cols_grad, whole_out, preferred_element_type=jnp.float32
    )
    hidden_grad = (hidden_up * hidden_slope).astype(jnp.bfloat16)
    grad_first = jnp.einsum(
        "scp,scj->pj", normed_cols, hidden_grad, preferred_element_type=jnp.float32
    )
    grad_second = jnp.einsum(
        "scp,scj->pj", mix_cols_grad, token_act, preferred_element_type=jnp.float32
    )
    token_sums = lax.psum_scatter(
        jnp.concatenate([grad_first, grad_second], axis=1),
        ("seq", "dp"),
        scatter_dimension=0,
        tiled=True,
    )
    grad_tok_in = token_sums[:, :width_hid]
    grad_tok_out = token_sums[:, width_hid:]
    normed_cols_grad = jnp.einsum(
        "scj,pj->scp", hidden_grad, whole_in, preferred_element_type=jnp.float32
    ).astype(jnp.bfloat16)
    normed_grad = to_patches(normed_cols_grad)
    grad_input = (
        middle_grad + norm_back(unit_first, scale_first, normed_grad.astype(jnp.float32))
    ).astype(jnp.bfloat16)
    return (grad_input, grad_tok_in, grad_tok_out, grad_ch_in, grad_ch_out)


def solution(mesh):
    in_specs = (
        P("dp", "seq", None),
        P("dp", "seq", None),
        P("seq", None),
        P("seq", None),
        P(),
        P(),
    )
    out_specs = (
        P("dp", "seq", None),
        P(("seq", "dp"), None),
        P(("seq", "dp"), None),
        P(("seq", "dp"), None),
        P(("seq", "dp"), None),
    )
    return jax.shard_map(local, mesh=mesh, in_specs=in_specs, out_specs=out_specs, check_vma=False)
```

profile of v0, /device:TPU:0, one launch (start us, length us, event | category | flops | bytes accessed | tf_op | source)
XLA Modules:
  0.0 1084.5 jit_solution(11490628716730762492)
XLA Ops:
  13.5 2.2 reshape.74
  15.7 24.4 %all_to_all.54 = bf16[32,2,4608]{2,1,0:T(2,128)(2,1)} all-to-all(bf16[32,2,4608]{2,1,0:T(2,128)(2,1)S(1)} %reshape.74), channel_id=1, replica_groups=mesh['seq'=32,'dp'=4] {'seq'}, dimensions={0} | all-to-all | bytes 1179648 | tf_op jit(solution)/shard_map/all_to_all | solution.py:34
  40.1 2.9 reshape.75
  43.0 3.2 copy.33
  48.3 49.3 %all-gather.3.cloned.1.call-done = bf16[2048,1024]{1,0:T(8,128)(2,1)} async-done(((bf16[64,1024]{1,0:T(8,128)(2,1)}), bf16[2048,1024]{1,0:T(8,128)(2,1)}) %all-gather.3.cloned.1.call-update) | async-done | bytes 4194320 | tf_op jit(solution)/shard_map/all_gather | solution.py:44
  97.7 3.8 fusion.6
  101.5 78.6 %all-gather.5.cloned.1.call-done = bf16[2048,1024]{1,0:T(8,128)(2,1)} async-done(((bf16[64,1024]{1,0:T(8,128)(2,1)}), bf16[2048,1024]{1,0:T(8,128)(2,1)}) %all-gather.5.cloned.1.call-update) | async-done | bytes 4194320 | tf_op jit(solution)/shard_map/all_gather | solution.py:45
  180.2 3.9 fusion.12
  184.1 4.2 copy.34
  188.2 6.0 reshape.76
  194.3 18.8 %all_to_all.55 = bf16[32,2,4608]{2,1,0:T(2,128)(2,1)} all-to-all(bf16[32,2,4608]{2,1,0:T(2,128)(2,1)S(1)} %reshape.76), channel_id=1, replica_groups=mesh['seq'=32,'dp'=4] {'seq'}, dimensions={0} | all-to-all | bytes 1179648 | tf_op jit(solution)/shard_map/all_to_all | solution.py:38
  213.0 6.9 reshape.77
  220.0 5.4 copy.35
  225.4 2.8 copy.36
  235.9 3.7 convolution_bitcast_fusion.3
  239.6 6.8 pad_maximum_fusion.1
  246.5 2.5 fusion.69
  252.8 18.4 %all_to_all.56 = bf16[32,2,4608]{2,1,0:T(2,128)(2,1)} all-to-all(bf16[32,2,4608]{2,1,0:T(2,128)(2,1)S(1)} %reshape.78), channel_id=1, replica_groups=mesh['seq'=32,'dp'=4] {'seq'}, dimensions={0} | all-to-all | bytes 1179648 | tf_op jit(solution)/shard_map/all_to_all | solution.py:34
  275.0 2.2 all_to_all.48
  277.2 3.5 fusion.38
  283.5 6.4 pad_maximum_fusion
  289.9 17.7 %copy.49 = f32[2048,2048]{1,0:T(8,128)} copy(f32[2048,2048]{0,1:T(8,128)} %pad_maximum_fusion) | data formatting | bytes 33554432
  307.6 3.7 fusion.9
  311.3 4.2 copy.40
  315.5 6.8 reshape.80
  322.2 4.5 all-to-all-start.3
  326.8 11.6 %all-to-all-done.3 = bf16[32,2,4608]{2,1,0:T(2,128)(2,1)S(1)} async-done(((bf16[32,2,4608]{2,1,0:T(2,128)(2,1)}), bf16[32,2,4608]{2,1,0:T(2,128)(2,1)S(1)}, u32[]{:S(2)}, u32[]{:S(2)}) %all-to-all-start.3) | async-done | bytes 589856 | tf_op jit(solution)/shard_map/all_to_all | solution.py:38
  338.4 5.7 reshape.81
  344.2 5.4 copy.41
  354.0 3.0 fusion.45
  357.1 53.7 %all-reduce.3.cloned.1.call-done = f32[1536,1536]{0,1:T(8,128)} async-done(((f32[1536,1536]{0,1:T(8,128)}), f32[1536,1536]{0,1:T(8,128)}) %all-reduce.3.cloned.1.call-update) | async-done | bytes 9437200
  413.9 662.5 %reduce-scatter.5.cloned.1.call-done = f32[16,2048]{1,0:T(8,128)} async-done(((f32[2048,2048]{1,0:T(8,128)}), f32[16,2048]{1,0:T(8,128)}) %reduce-scatter.5.cloned.1.call-update) | async-done | bytes 131088
  (74 shorter events, 35.5 us)
Async XLA Ops:
  7.2 222.8 %copy-start = (bf16[1536,768]{1,0:T(8,128)(2,1)S(1)}, bf16[1536,768]{1,0:T(8,128)(2,1)}, u32[]{:S(2)}) copy-start(bf16[1536,768]{1,0:T(8,128)(2,1)} %param.10) | copy-start | bytes 7077892
  7.2 4.1 copy-start.2
  7.2 90.5 %all-gather.3.cloned.1.call-start = ((), (), s32[]{:S(2)}) async-start(), calls=%async_computation.5 | async-start | bytes 4325376 | tf_op jit(solution)/shard_map/all_gather | solution.py:44
  7.9 172.2 %all-gather.5.cloned.1.call-start = ((), (), s32[]{:S(2)}) async-start(), calls=%async_computation.6 | async-start | bytes 4325376 | tf_op jit(solution)/shard_map/all_gather | solution.py:45
  8.7 402.0 %all-reduce.3.cloned.1.call-start = ((), (), s32[]{:S(2)}) async-start(), calls=%async_computation.8 | async-start | bytes 18874368
  48.3 53.2 %copy-start.4 = (bf16[6,24,2048]{2,1,0:T(8,128)(2,1)}, bf16[6,24,2048]{2,1,0:T(8,128)(2,1)S(1)}, u32[]{:S(2)}) copy-start(bf16[6,24,2048]{2,1,0:T(8,128)(2,1)S(1)} %all_to_all.43) | copy-start | bytes 1769476
  230.0 1.2 copy-start.8
  231.2 1.7 copy-start.16
  234.9 1.0 copy-start.17
  246.4 830.0 %reduce-scatter.5.cloned.1.call-start = ((), (), s32[]{:S(2)}) async-start(), calls=%async_computation.7 | async-start | bytes 16908288
  246.5 3.6 copy-start.9
  249.0 1.1 copy-start.6
  249.0 2.6 copy-start.12
  249.0 2.6 copy-start.14
  275.0 2.3 copy-start.11
  277.2 3.5 copy-start.5
  322.2 16.2 %all-to-all-start.3 = ((bf16[32,2,4608]{2,1,0:T(2,128)(2,1)}), bf16[32,2,4608]{2,1,0:T(2,128)(2,1)S(1)}, u32[]{:S(2)}, u32[]{:S(2)}) async-start(bf16[32,2,4608]{2,1,0:T(2,128)(2,1)} %reshape.80), calls=%async_computation.3 | async-start | bytes 1179648 | tf_op jit(solution)/shard_map/all_to_all | solution.py:38
  351.6 1.0 copy-start.3
  352.6 1.3 copy-start.7
  352.6 1.4 copy-start.10
  352.6 1.4 copy-start.13
  352.6 1.4 copy-start.15
  354.0 724.0 %copy-start.1 = (bf16[1536,768]{1,0:T(8,128)(2,1)S(1)}, bf16[1536,768]{1,0:T(8,128)(2,1)}, u32[]{:S(2)}) copy-start(bf16[1536,768]{1,0:T(8,128)(2,1)} %param.10) | copy-start | bytes 7077892
Sparse Core Ops, SparseCore 0:
  11.2 86.4 all-gather.2
  100.8 79.2 all-gather.4
  246.5 164.1 all-reduce.2
  413.0 663.4 reduce-scatter.4
where the time goes:
time: 1090 us; the launch traced here: 1080 us
  waiting for transfers between devices  857 us (79%)
  local copies, waits for them, and re-layouts  96.5 us (9%)
  blocking collectives  61.6 us (6%)
  matrix products  28.6 us (3%)
  other arithmetic  21.7 us (2%)
  between operations  14.2 us (1%)
    unnamed x6, waiting for transfers between devices  718 us
    all_gather x1, waiting for transfers between devices, local(): lax.all_gather(tok_out_w, 'seq', axis=0, tiled=True)  78.6 us
    unnamed x47, local copies, waits for them, and re-layouts  57 us
    all_gather x1, waiting for transfers between devices, local(): lax.all_gather(tok_in_w, 'seq', axis=0, tiled=True)  49.3 us
    all_to_all x2, blocking collectives, to_channels(): lax.all_to_all(flipped, 'seq', split_axis=1, concat_axis=2, tiled=True)  42.8 us
  transfers between devices with their start and end apart: 5, of which 5 were waited for; matrix products, arithmetic and copies ran while one was open for 8% of the time, Pallas kernels for 0%

commit v1 on v0

v1 whole, which is shorter than its diff:
```python
import functools
import math

import jax
import jax.numpy as jnp
from jax import lax
from jax.experimental import pallas as pl
from jax.experimental.pallas import tpu as pltpu
from jax.sharding import PartitionSpec as P

BF = jnp.bfloat16
F32 = jnp.float32
MESH = pl.DeviceIdType.MESH
ANY = pl.BlockSpec(memory_space=pl.ANY)
LANES = 128


def normalize(values):
    center = values - jnp.mean(values, axis=-1, keepdims=True)
    inv_scale = lax.rsqrt(jnp.mean(center * center, axis=-1, keepdims=True) + 1e-05)
    return (center * inv_scale, inv_scale)


def norm_back(unit, inv_scale, upstream):
    first = jnp.mean(upstream, axis=-1, keepdims=True)
    second = jnp.mean(upstream * unit, axis=-1, keepdims=True)
    return inv_scale * (upstream - first - unit * second)


def gelu_pair(values):
    factor = math.sqrt(2.0 / math.pi)
    inner = factor * (values + 0.044715 * values * values * values)
    tangent = jnp.tanh(inner)
    result = 0.5 * values * (1.0 + tangent)
    slope = 0.5 * (1.0 + tangent) + 0.5 * values * (1.0 - tangent * tangent) * factor * (
        1.0 + 3.0 * 0.044715 * values * values
    )
    return (result, slope)


class Here:
    def __init__(self):
        self.q = lax.axis_index("seq")
        self.d = lax.axis_index("dp")
        self.y = self.q // 8
        self.xh = (self.q // 4) % 2
        self.z = self.q % 4
        self.xl = self.d // 2
        self.c = self.d % 2
        self.x = self.xh * 2 + self.xl

    def at(self, x=None, y=None, z=None, c=None):
        x = self.x if x is None else x
        y = self.y if y is None else y
        z = self.z if z is None else z
        c = self.c if c is None else c
        return {"seq": (y * 2 + x // 2) * 4 + z, "dp": (x % 2) * 2 + c}

    def peer(self, q):
        return {"seq": q, "dp": self.d}

    def sibling(self):
        return {"seq": self.q, "dp": self.d + 1 - 2 * self.c}

    def extra_of(self, e):
        return 8 * e + ((e + self.d // 2) % 2) * 4 + (e + self.d) % 4

    def has_extra(self):
        return self.q == self.extra_of(self.y)


def remote(src, dst, send, recv, device):
    return pltpu.make_async_remote_copy(
        src_ref=src, dst_ref=dst, send_sem=send, recv_sem=recv,
        device_id=device, device_id_type=MESH,
    )


def drain(ref, sem):
    pltpu.make_async_copy(ref, ref, sem).wait()


def greet(devices):
    barrier = pltpu.get_barrier_semaphore()
    for device in devices:
        pl.semaphore_signal(barrier, inc=1, device_id=device, device_id_type=MESH)
    return len(devices)


def greet_seq(here):
    barrier = pltpu.get_barrier_semaphore()

    def body(i, carry):
        pl.semaphore_signal(
            barrier, inc=1, device_id=here.peer((here.q + i) % 32), device_id_type=MESH
        )
        return carry

    lax.fori_loop(1, 32, body, 0)
    return 31


def rows(start, size):
    return pl.ds(pl.multiple_of(start * size, size), size)


def tile_of(ref, s, b):
    return ref.at[rows(s, 64), pl.ds(pl.multiple_of(b * LANES, LANES), LANES)]


def send_to_channels(here, src, cols, zero, sems):
    send, recv, own, esend, erecv = sems
    mine = rows(here.q, 64)

    def body(i, carry):
        dest = (here.q + i) % 32
        remote(
            tile_of(src, dest // 6, dest % 6), cols.at[mine, pl.ds(0, LANES)],
            send, recv, here.peer(dest),
        ).start()
        return carry

    lax.fori_loop(1, 32, body, 0)
    pltpu.make_async_copy(
        tile_of(src, here.q // 6, here.q % 6), cols.at[mine, pl.ds(0, LANES)], own
    ).start()
    for e in range(4):
        dest = here.extra_of(e)
        block = tile_of(src, 5, 2 + e)
        place = cols.at[mine, pl.ds(LANES, LANES)]

        @pl.when(dest != here.q)
        def _():
            remote(block, place, esend.at[e], erecv, here.peer(dest)).start()

        @pl.when(dest == here.q)
        def _():
            pltpu.make_async_copy(block, place, esend.at[e]).start()

    @pl.when(jnp.logical_not(here.has_extra()))
    def _():
        zero[...] = jnp.zeros_like(zero)
        for k in range(8):
            pltpu.make_async_copy(
                zero, cols.at[pl.ds(k * 256, 256), pl.ds(LANES, LANES)], erecv
            ).start()


def wait_to_channels(here, src, cols, zero, sems):
    send, recv, own, esend, erecv = sems
    many = cols.at[pl.ds(0, 31 * 64), pl.ds(0, LANES)]
    drain(many, send)
    drain(many, recv)
    drain(cols.at[pl.ds(0, 64), pl.ds(0, LANES)], own)
    for e in range(4):
        drain(cols.at[pl.ds(0, 64), pl.ds(0, LANES)], esend.at[e])

    @pl.when(here.has_extra())
    def _():
        drain(cols.at[pl.ds(0, 31 * 64), pl.ds(LANES, LANES)], erecv)

    @pl.when(jnp.logical_not(here.has_extra()))
    def _():
        drain(cols.at[:, pl.ds(LANES, LANES)], erecv)


CHANNEL_SEMS = [
    pltpu.SemaphoreType.DMA, pltpu.SemaphoreType.DMA, pltpu.SemaphoreType.DMA,
    pltpu.SemaphoreType.DMA((4,)), pltpu.SemaphoreType.DMA,
]


def send_to_patches(here, cols, out, sems):
    send, recv, own, esend, erecv = sems
    place = tile_of(out, here.q // 6, here.q % 6)
    place_extra = tile_of(out, 5, 2 + here.y)

    def body(i, carry):
        dest = (here.q + i) % 32
        remote(
            cols.at[rows(dest, 64), pl.ds(0, LANES)], place, send, recv, here.peer(dest)
        ).start()
        return carry

    lax.fori_loop(1, 32, body, 0)
    pltpu.make_async_copy(cols.at[rows(here.q, 64), pl.ds(0, LANES)], place, own).start()

    @pl.when(here.has_extra())
    def _():
        def more(i, carry):
            dest = (here.q + i) % 32
            remote(
                cols.at[rows(dest, 64), pl.ds(LANES, LANES)], place_extra,
                esend, erecv.at[here.y], here.peer(dest),
            ).start()
            return carry

        lax.fori_loop(1, 32, more, 0)
        pltpu.make_async_copy(
            cols.at[rows(here.q, 64), pl.ds(LANES, LANES)], place_extra, erecv.at[here.y]
        ).start()


def wait_to_patches(here, cols, out, sems):
    send, recv, own, esend, erecv = sems
    many = cols.at[pl.ds(0, 31 * 64), pl.ds(0, LANES)]
    one = cols.at[pl.ds(0, 64), pl.ds(0, LANES)]
    drain(many, send)
    drain(many, recv)
    drain(one, own)
    for e in range(4):
        drain(one, erecv.at[e])

    @pl.when(here.has_extra())
    def _():
        drain(many, esend)


PATCH_SEMS = [
    pltpu.SemaphoreType.DMA, pltpu.SemaphoreType.DMA, pltpu.SemaphoreType.DMA,
    pltpu.SemaphoreType.DMA, pltpu.SemaphoreType.DMA((4,)),
]


def params(cid, vmem=None):
    return pltpu.CompilerParams(
        collective_id=cid, has_side_effects=True, vmem_limit_bytes=vmem
    )


def to_channels_kernel(src, cols, zero, *sems):
    here = Here()
    pl.semaphore_wait(pltpu.get_barrier_semaphore(), greet_seq(here))
    send_to_channels(here, src, cols, zero, sems)
    wait_to_channels(here, src, cols, zero, sems)


def to_channels(values, cid):
    return pl.pallas_call(
        to_channels_kernel,
        out_shape=jax.ShapeDtypeStruct((2048, 2 * LANES), BF),
        in_specs=[ANY], out_specs=ANY,
        scratch_shapes=[pltpu.VMEM((256, LANES), BF)] + CHANNEL_SEMS,
        compiler_params=params(cid),
        name="to_channels",
    )(values)


def to_patches_kernel(cols, out, *sems):
    here = Here()
    pl.semaphore_wait(pltpu.get_barrier_semaphore(), greet_seq(here))
    send_to_patches(here, cols, out, sems)
    wait_to_patches(here, cols, out, sems)


def to_patches(cols, cid):
    return pl.pallas_call(
        to_patches_kernel,
        out_shape=jax.ShapeDtypeStruct((384, 768), BF),
        in_specs=[ANY], out_specs=ANY,
        scratch_shapes=PATCH_SEMS,
        compiler_params=params(cid),
        name="to_patches",
    )(cols)


def gather_kernel(src, w_in, w_out, cols, full_in, full_out, zero, *sems):
    a2a, (own, send, recv, bsend, brecv) = sems[:5], sems[5:]
    here = Here()
    c, y, xh, z = here.c, here.y, here.xh, here.z
    sib = here.sibling()
    count = greet_seq(here) + greet([sib])
    pl.semaphore_wait(pltpu.get_barrier_semaphore(), count)

    fulls = (full_in, full_out)
    started = []

    def push(w, k, ref, device):
        copy = remote(ref, ref, send.at[w, k], recv.at[w, k], device)
        copy.start()
        started.append(copy)
        return copy

    def share(w, k, ref):
        copy = remote(ref, ref, bsend.at[w, k], brecv.at[w, k], sib)
        copy.start()
        started.append(copy)

    locals_ = []
    crossing = []
    for w, part in enumerate((w_in, w_out)):
        copy = pltpu.make_async_copy(part, fulls[w].at[y, xh, z], own.at[w])
        copy.start()
        locals_.append(copy)
        copy = remote(
            part.at[c], fulls[w].at[y, xh, z, c], send.at[w, 0], recv.at[w, 0],
            here.at(x=(here.x + 2) % 4),
        )
        copy.start()
        crossing.append(copy)
    send_to_channels(here, src, cols, zero, a2a)

    def chunk(w, stage, pos, half=None):
        h = slice(None) if half is None else half
        along_z = (stage == 0) == (w == 0)
        if along_z:
            if stage == 0:
                return fulls[w].at[y, h, pos, c]
            return fulls[w].at[:, h, pos, c]
        if stage == 0:
            return fulls[w].at[pos, h, z, c]
        return fulls[w].at[pos, h, :, c]

    for w in range(2):
        locals_[w].wait()
        crossing[w].wait_recv()
        share(w, 0, fulls[w].at[y, 1 - xh, z, c])
    for stage in range(2):
        base = 1 + 4 * stage
        legs = []
        for w in range(2):
            along_z = (stage == 0) == (w == 0)
            me = z if along_z else y
            up, down = (me + 1) % 4, (me + 3) % 4
            far = (me + 2) % 4
            if along_z:
                to_up, to_down = here.at(z=up), here.at(z=down)
            else:
                to_up, to_down = here.at(y=up), here.at(y=down)
            rise = push(w, base, chunk(w, stage, me), to_up)
            fall = push(w, base + 1, chunk(w, stage, me), to_down)
            legs.append((up, down, far, to_up, to_down, rise, fall))
        late = []
        for w in range(2):
            up, down, far, to_up, to_down, rise, fall = legs[w]
            rise.wait_recv()
            one = push(w, base + 2, chunk(w, stage, down, 0), to_up)
            share(w, base, chunk(w, stage, down))
            fall.wait_recv()
            two = push(w, base + 3, chunk(w, stage, up, 1), to_down)
            share(w, base + 1, chunk(w, stage, up))
            late.append((one, two))
        for w in range(2):
            far = legs[w][2]
            late[w][0].wait_recv()
            share(w, base + 2, chunk(w, stage, far, 0))
            late[w][1].wait_recv()
            share(w, base + 3, chunk(w, stage, far, 1))

    for w in range(2):
        crossing[w].wait_send()
    for copy in started:
        copy.wait_send()
    other = 1 - c
    for w in range(2):
        def theirs(stage, pos, half=None):
            h = slice(None) if half is None else half
            along_z = (stage == 0) == (w == 0)
            if along_z:
                return fulls[w].at[y, h, pos, other] if stage == 0 else fulls[w].at[:, h, pos, other]
            return fulls[w].at[pos, h, z, other] if stage == 0 else fulls[w].at[pos, h, :, other]

        drain(fulls[w].at[y, 1 - xh, z, other], brecv.at[w, 0])
        for stage in range(2):
            along_z = (stage == 0) == (w == 0)
            me = z if along_z else y
            base = 1 + 4 * stage
            drain(theirs(stage, (me + 3) % 4), brecv.at[w, base])
            drain(theirs(stage, (me + 1) % 4), brecv.at[w, base + 1])
            drain(theirs(stage, (me + 2) % 4, 0), brecv.at[w, base + 2])
            drain(theirs(stage, (me + 2) % 4, 1), brecv.at[w, base + 3])
    wait_to_channels(here, src, cols, zero, a2a)


def gather(values, w_in, w_out, cid):
    full = jax.ShapeDtypeStruct((4, 2, 4, 2, 32, 1024), BF)
    return pl.pallas_call(
        gather_kernel,
        out_shape=(jax.ShapeDtypeStruct((2048, 2 * LANES), BF), full, full),
        in_specs=[ANY] * 3, out_specs=(ANY,) * 3,
        scratch_shapes=[pltpu.VMEM((256, LANES), BF)] + CHANNEL_SEMS + [
            pltpu.SemaphoreType.DMA((2,)),
            pltpu.SemaphoreType.DMA((2, 9)), pltpu.SemaphoreType.DMA((2, 9)),
            pltpu.SemaphoreType.DMA((2, 9)), pltpu.SemaphoreType.DMA((2, 9)),
        ],
        compiler_params=params(cid),
        name="gather_and_to_channels",
    )(values, w_in.reshape(2, 32, 1024), w_out.reshape(2, 32, 1024))


ORDERS = ("yzx", "zxy", "xyz")


def add_into(target, other):
    lead = target.shape[:-2]
    count = math.prod(lead)

    def body(i, carry):
        index = []
        rest = i
        for size in reversed(lead):
            index.append(rest % size)
            rest = rest // size
        index = tuple(reversed(index))
        target[index] = (target[index].astype(F32) + other[index].astype(F32)).astype(BF)
        return carry

    if count == 1:
        index = (0,) * len(lead)
        target[index] = (target[index].astype(F32) + other[index].astype(F32)).astype(BF)
    else:
        lax.fori_loop(0, count, body, 0)


def sums_kernel(g0, g1, g2, cols, o0, o1, o2, patches, *scratch):
    here = Here()
    c = here.c
    acc, pair = scratch[0:3], scratch[3:6]
    bufs = [scratch[6 + 12 * p:18 + 12 * p] for p in range(3)]
    last = scratch[42]
    lsem, psend, precv, send, recv, fsem = scratch[43:49]
    a2a = scratch[49:54]
    sib = here.sibling()
    near = []
    for k in (1, 2, 3):
        near += [here.at(x=(here.x + k) % 4), here.at(y=(here.y + k) % 4), here.at(z=(here.z + k) % 4)]
    count = greet_seq(here) + greet(
        [sib, here.at(x=(here.x + 1) % 4), here.at(x=(here.x + 3) % 4)]
    )
    pl.semaphore_wait(pltpu.get_barrier_semaphore(), count)

    def side(p, ref, which):
        if p < 2:
            return ref.at[:, :, :, :, which]
        return ref.at[:, :, :, :, :, pl.ds(pl.multiple_of(which * 384, 384), 384)]

    ins = (g0, g1, g2)
    loads, pairs = [], []
    send_to_patches(here, cols, patches, a2a)
    for p in range(3):
        pairs.append(remote(side(p, ins[p], 1 - c), pair[p], psend.at[p], precv.at[p], sib))
        pairs[p].start()
        loads.append(pltpu.make_async_copy(side(p, ins[p], c), acc[p], lsem.at[p]))
        loads[p].start()

    def axis(p, stage):
        name = ORDERS[p][stage]
        me = getattr(here, name)
        up, down = (me + 1) % 4, (me + 3) % 4
        return name, me, up, down, here.at(**{name: up}), here.at(**{name: down})

    def chunk(p, stage, pos, half=None):
        done = ORDERS[p][:stage]
        name = ORDERS[p][stage]
        index = {"y": slice(None), "xh": slice(None), "z": slice(None), "xl": slice(None)}
        for other in done:
            if other == "x":
                index["xh"], index["xl"] = here.xh, here.xl
            else:
                index[other] = getattr(here, other)
        if name == "x":
            index["xh"], index["xl"] = pos // 2, pos % 2
        else:
            index[name] = pos
        tail = []
        if half is not None:
            for other in ("y", "xh", "z", "xl"):
                if isinstance(index[other], slice):
                    size = {"y": 4, "xh": 2, "z": 4, "xl": 2}[other]
                    index[other] = pl.ds(half * (size // 2), size // 2)
                    break
            else:
                width = acc[p].shape[-1]
                if width == 1024:
                    tail = [slice(None), pl.ds(half * 512, 512)]
                else:
                    tail = [pl.ds(16 * half, 16 + 16 * half)]
        return acc[p].at[tuple([index["y"], index["xh"], index["z"], index["xl"]] + tail)]

    waits = []
    for p in range(3):
        loads[p].wait()
        pairs[p].wait_recv()
        add_into(acc[p], pair[p])
        waits.append(pairs[p])

    for stage in range(3):
        first = []
        for p in range(3):
            name, me, up, down, to_up, to_down = axis(p, stage)
            a, b, f, g = bufs[p][4 * stage:4 * stage + 4]
            far = (me + 2) % 4
            k = 4 * stage
            one = remote(chunk(p, stage, far, 0), a, send.at[p, k], recv.at[p, k], to_up)
            one.start()
            two = remote(chunk(p, stage, far, 1), b, send.at[p, k + 1], recv.at[p, k + 1], to_down)
            two.start()
            first.append((one, two))
        second = []
        for p in range(3):
            name, me, up, down, to_up, to_down = axis(p, stage)
            a, b, f, g = bufs[p][4 * stage:4 * stage + 4]
            k = 4 * stage
            first[p][0].wait_recv()
            add_into(chunk(p, stage, up, 0), a)
            three = remote(chunk(p, stage, up), f, send.at[p, k + 2], recv.at[p, k + 2], to_up)
            three.start()
            first[p][1].wait_recv()
            add_into(chunk(p, stage, down, 1), b)
            four = remote(chunk(p, stage, down), g, send.at[p, k + 3], recv.at[p, k + 3], to_down)
            four.start()
            second.append((three, four))
            waits += [first[p][0], first[p][1], three, four]
        for p in range(3):
            name, me, up, down, to_up, to_down = axis(p, stage)
            a, b, f, g = bufs[p][4 * stage:4 * stage + 4]
            second[p][0].wait_recv()
            second[p][1].wait_recv()
            mine = chunk(p, stage, me)
            if stage < 2:
                add_into(mine, f)
                add_into(mine, g)
            else:
                total = mine[...].astype(F32) + f[...].astype(F32) + g[...].astype(F32)
                if p < 2:
                    (o0, o1)[p][...] = total
                else:
                    last[c] = total
    swap = remote(last.at[c], last.at[c], fsem.at[0], fsem.at[1], sib)
    swap.start()
    for copy in waits:
        copy.wait_send()
    swap.wait()
    o2[:, 0:384] = last[0]
    o2[:, 384:768] = last[1]
    wait_to_patches(here, cols, patches, a2a)


def sums(g_in, g_out, g_chan, cols, cid):
    scratch = []
    tails = ((16, 1024), (16, 1024), (48, 384))
    for _ in range(2):
        scratch += [pltpu.VMEM((4, 2, 4, 2) + tail, BF) for tail in tails]
    for p in range(3):
        for stage in range(3):
            dims = {"y": 4, "xh": 2, "z": 4, "xl": 2}
            for name in ORDERS[p][:stage + 1]:
                for key in {"x": ("xh", "xl"), "y": ("y",), "z": ("z",)}[name]:
                    del dims[key]
            lead = list(dims.values())
            tail = list(tails[p])
            if lead:
                half = [lead[0] // 2] + lead[1:] + tail
                halves = (half, half)
            elif p < 2:
                halves = ([16, 512], [16, 512])
            else:
                halves = ([16, 384], [32, 384])
            scratch += [pltpu.VMEM(tuple(h), BF) for h in halves]
            scratch += [pltpu.VMEM(tuple(lead + tail), BF)] * 2
    scratch += [pltpu.VMEM((2, 48, 384), F32)]
    dma = pltpu.SemaphoreType.DMA
    scratch += [dma((3,)), dma((3,)), dma((3,)), dma((3, 12)), dma((3, 12)), dma((2,))]
    scratch += PATCH_SEMS
    vmem = pl.BlockSpec(memory_space=pltpu.VMEM)
    return pl.pallas_call(
        sums_kernel,
        out_shape=(
            jax.ShapeDtypeStruct((16, 1024), F32),
            jax.ShapeDtypeStruct((16, 1024), F32),
            jax.ShapeDtypeStruct((48, 768), F32),
            jax.ShapeDtypeStruct((384, 768), BF),
        ),
        in_specs=[ANY] * 4, out_specs=(vmem, vmem, vmem, ANY),
        scratch_shapes=scratch,
        compiler_params=params(cid, 48 * 1024 * 1024),
        name="sums_and_to_patches",
    )(
        g_in.reshape(4, 2, 4, 2, 2, 16, 1024),
        g_out.reshape(4, 2, 4, 2, 2, 16, 1024),
        g_chan.reshape(4, 2, 4, 2, 48, 768),
        cols,
    )


def local(spectra_in, cotangent, tok_in_w, tok_out_w, ch_in_w, ch_out_w):
    source = spectra_in.reshape(384, 768).astype(F32)
    cotangent = cotangent.reshape(384, 768)
    unit_first, scale_first = normalize(source)
    normed = unit_first.astype(BF)
    normed_cols, whole_in, whole_out = gather(normed, tok_in_w, tok_out_w, 0)
    whole_in = whole_in.reshape(2048, 1024)
    whole_out = whole_out.reshape(2048, 1024)
    hidden = jnp.einsum("pc,pj->cj", normed_cols, whole_in, preferred_element_type=F32)
    hidden_val, hidden_slope = gelu_pair(hidden)
    token_act = hidden_val.astype(BF)
    mix_cols = jnp.einsum("pj,cj->pc", whole_out, token_act, preferred_element_type=F32).astype(BF)
    token_mix = to_patches(mix_cols, 1)
    middle = (source + token_mix.astype(F32)).astype(BF)
    unit_second, scale_second = normalize(middle.astype(F32))
    normed_second = unit_second.astype(BF)
    chan_pre = jnp.einsum("tc,hc->th", normed_second, ch_in_w, preferred_element_type=F32)
    chan_val, chan_slope = gelu_pair(chan_pre)
    chan_act = chan_val.astype(BF)
    chan_down = jnp.einsum("tc,hc->th", cotangent, ch_out_w, preferred_element_type=F32)
    chan_grad = (chan_down * chan_slope).astype(BF)
    second_up = jnp.einsum("th,hc->tc", chan_grad, ch_in_w, preferred_element_type=F32)
    middle_grad = cotangent.astype(F32) + norm_back(unit_second, scale_second, second_up)
    mix_grad = middle_grad.astype(BF)
    mix_cols_grad = to_channels(mix_grad, 2)
    grad_up = jnp.einsum("th,tc->hc", chan_grad, normed_second, preferred_element_type=F32).astype(BF)
    grad_down = jnp.einsum("th,tc->hc", chan_act, cotangent, preferred_element_type=F32).astype(BF)
    g_chan = jnp.concatenate([grad_up.reshape(64, 24, 768), grad_down.reshape(64, 24, 768)], axis=1)
    hidden_up = jnp.einsum("pc,pj->cj", mix_cols_grad, whole_out, preferred_element_type=F32)
    hidden_grad = (hidden_up * hidden_slope).astype(BF)
    grad_first = jnp.einsum("pc,cj->pj", normed_cols, hidden_grad, preferred_element_type=F32).astype(BF)
    grad_second = jnp.einsum("pc,cj->pj", mix_cols_grad, token_act, preferred_element_type=F32).astype(BF)
    normed_cols_grad = jnp.einsum(
        "pj,cj->pc", whole_in, hidden_grad, preferred_element_type=F32
    ).astype(BF)
    grad_tok_in, grad_tok_out, both, normed_grad = sums(
        grad_first, grad_second, g_chan, normed_cols_grad, 3
    )
    core = lax.axis_index("dp") % 2
    grad_ch_in = lax.dynamic_slice_in_dim(both, 12 * core, 12, 0)
    grad_ch_out = lax.dynamic_slice_in_dim(both, 24 + 12 * core, 12, 0)
    grad_input = (
        middle_grad + norm_back(unit_first, scale_first, normed_grad.astype(F32))
    ).astype(BF)
    return (grad_input.reshape(6, 64, 768), grad_tok_in, grad_tok_out, grad_ch_in, grad_ch_out)


def solution(mesh):
    in_specs = (
        P("dp", "seq", None),
        P("dp", "seq", None),
        P("seq", None),
        P("seq", None),
        P(),
        P(),
    )
    out_specs = (
        P("dp", "seq", None),
        P(("seq", "dp"), None),
        P(("seq", "dp"), None),
        P(("seq", "dp"), None),
        P(("seq", "dp"), None),
    )
    return jax.shard_map(local, mesh=mesh, in_specs=in_specs, out_specs=out_specs, check_vma=False)
```

time: 1090 us -> 191 us (0.18)
  waiting for transfers between devices: 857 us -> 0 us
  Pallas kernels: 0 us -> 146 us
  local copies, waits for them, and re-layouts: 96.5 us -> 3.86 us
  blocking collectives: 61.6 us -> 0 us
  between operations: 14.2 us -> 0.9 us
    unnamed x6 -> x0, waiting for transfers between devices: 718 us -> none
    pallas_call x0 -> x4, Pallas kernels: none -> 146 us  [the longest x1 62.1 us: sums(): pl.pallas_call(sums_kernel, out_shape=(jax.ShapeDtypeStruct((16, 1024), F...]
    all_gather x2 -> x0, waiting for transfers between devices: 128 us -> none  [the longest x1 78.6 us: local(): lax.all_gather(tok_out_w, 'seq', axis=0, tiled=True)]
    all_to_all x3 -> x0, blocking collectives: 61.6 us -> none  [the longest x2 42.8 us: to_channels(): lax.all_to_all(flipped, 'seq', split_axis=1, concat_axis=2, tiled=True)]
    unnamed x47 -> x30, local copies, waits for them, and re-layouts: 57 us -> 3.06 us
    convert_element_type x6 -> x0, local copies, waits for them, and re-layouts: 24 us -> none  [the longest x2 8.21 us: local(): middle = (source + token_mix.astype(jnp.float32)).astype(jnp.bfloat16)]
    all_to_all x1 -> x0, waiting for transfers between devices: 11.6 us -> none  [to_patches(): lax.all_to_all(channel_major, 'seq', split_axis=2, concat_axis=1, tiled=T...]
  transfers between devices with their start and end apart: 5 -> 0, of which waited for: 5 -> 0; matrix products, arithmetic and copies ran while one was open for 8% -> 0% of each run, Pallas kernels for 0% -> 0%
where the time goes in v1:
time: 191 us; the launch traced here: 190 us
  Pallas kernels  146 us (76%)
  matrix products  26.2 us (14%)
  other arithmetic  12.7 us (7%)
  local copies, waits for them, and re-layouts  3.86 us (2%)
    pallas_call x1, Pallas kernels, sums(): pl.pallas_call(sums_kernel, out_shape=(jax.ShapeDtypeStruct((16, 1024), F...  62.1 us
    pallas_call x1, Pallas kernels, gather(): pl.pallas_call(gather_kernel, out_shape=(jax.ShapeDtypeStruct((2048, 2 *...  51.3 us
    pallas_call x1, Pallas kernels, to_channels(): pl.pallas_call(to_channels_kernel, out_shape=jax.ShapeDtypeStruct((2048,...  16.9 us
    pallas_call x1, Pallas kernels, to_patches(): pl.pallas_call(to_patches_kernel, out_shape=jax.ShapeDtypeStruct((384, 76...  15.9 us
    dot_general x1, matrix products, local(): jnp.einsum('pc,pj->cj', mix_cols_grad, whole_out, preferred_element_type=...  4.67 us
    dot_general x1, matrix products, local(): jnp.einsum('pc,pj->cj', normed_cols, whole_in, preferred_element_type=F32)  3.93 us

profile of v1, /device:TPU:0, one launch (start us, length us, event | category | flops | bytes accessed | tf_op | source)
XLA Modules:
  0.0 189.8 jit_solution(12932437031539261008)
XLA Ops:
  0.7 1.4 convert_reduce_fusion.2
  2.0 0.1 div.27
  2.1 1.3 fusion.23
  3.5 0.1 rsqrt.20
  3.6 2.1 %fusion.26.src = bf16[384,768]{1,0:T(8,128)(2,1)} fusion(bf16[6,64,768]{2,1,0:T(8,128)(2,1)} %param.6, f32[384]{0:T(512)S(1)} %rsqrt.20, f32[384]{0:T(512)S(1)} %div.27), kind=kLoop, calls=%fused_computation.49 | loop fusion | flops 1179648 | bytes 1182720 | tf_op jit(solution)/shard_map/convert_element_type | solution.py:590
  5.7 51.3 %gather_and_to_channels.1 = (bf16[2048,256]{1,0:T(8,128)(2,1)}, bf16[4,2,4,2,32,1024]{5,4,3,2,1,0:T(8,128)(2,1)}, bf16[4,2,4,2,32,1024]{5,4,3,2,1,0:T(8,128)(2,1)}) custom-call(bf16[384,768]{1,0:T(8,128)(2,1)} %fusion.26.src, bf16[2,32,1024]{2,1,0:T(8,128)(2,1)} %bitcast.52, bf16[2,32,1024]{2,1,0:T(8,128)(2,1)} %bitcast.53), custom_call_target="tpu_custom_call" | custom-call | tf_op jit(solution)/shard_map/gather_and_to_channels/pallas_call | solution.py:377
  57.0 3.9 %fusion.48 = f32[256,1024]{1,0:T(8,128)S(1)} fusion(bf16[2048,256]{1,0:T(8,128)(2,1)} %get-tuple-element.13, bf16[2048,1024]{1,0:T(8,128)(2,1)} %bitcast.54), kind=kOutput, calls=%fused_computation.78 | convolution fusion | flops 1073741824 | bytes 6291456 | tf_op jit(solution)/shard_map/pc,pj->cj/dot_general | solution.py:594
  61.0 1.0 copy-done.6
  61.9 2.5 %convolution_convert_fusion.5.cols = bf16[2048,256]{1,0:T(8,128)(2,1)} fusion(bf16[2048,1024]{1,0:T(8,128)(2,1)S(1)} %bitcast.57, f32[256,1024]{1,0:T(8,128)S(1)} %fusion.48), kind=kOutput, calls=%fused_computation.10 | convolution fusion | flops 1076625408 | bytes 6291456 | tf_op jit(solution)/shard_map/pj,cj->pc/dot_general | solution.py:597
  64.5 15.9 %to_patches.1 = bf16[384,768]{1,0:T(8,128)(2,1)} custom-call(bf16[2048,256]{1,0:T(8,128)(2,1)} %convolution_convert_fusion.5.cols), custom_call_target="tpu_custom_call" | custom-call | tf_op jit(solution)/shard_map/to_patches/pallas_call | solution.py:257
  80.4 1.3 convert_reduce_fusion.1
  81.7 0.3 fusion.16
  82.0 1.2 fusion.42
  83.2 0.7 copy-done.11
  83.9 2.0 %fusion = bf16[384,1536]{1,0:T(8,128)(2,1)S(1)} fusion(bf16[384,768]{1,0:T(8,128)(2,1)S(1)} %bitcast.49, bf16[1536,768]{1,0:T(8,128)(2,1)S(1)} %copy-done.11, f32[384,1536]{1,0:T(8,128)S(1)} %fusion.42), kind=kOutput, calls=%fused_computation.8 | convolution fusion | flops 917176320 | bytes 6488064 | tf_op jit(solution)/shard_map/tc,hc->th/dot_general | solution.py:605
  85.9 3.1 %convolution_convert_fusion.2 = bf16[1536,768]{1,0:T(8,128)(2,1)} fusion(bf16[384,768]{1,0:T(8,128)(2,1)S(1)} %bitcast.50, f32[384,1536]{1,0:T(8,128)S(1)} %fusion.42), kind=kOutput, calls=%fused_computation.5 | convolution fusion | flops 912457728 | bytes 5308416 | tf_op jit(solution)/shard_map/th,tc->hc/dot_general | solution.py:612
  89.0 1.2 fusion.44
  90.2 1.7 fusion.45
  91.9 16.9 %to_channels.1 = bf16[2048,256]{1,0:T(8,128)(2,1)} custom-call(bf16[384,768]{1,0:T(8,128)(2,1)} %get-tuple-element.23.src), custom_call_target="tpu_custom_call" | custom-call | tf_op jit(solution)/shard_map/to_channels/pallas_call | solution.py:239
  108.8 4.7 %fusion.11 = bf16[256,1024]{1,0:T(8,128)(2,1)S(1)} fusion(bf16[2048,256]{1,0:T(8,128)(2,1)} %to_channels.1, bf16[2048,1024]{1,0:T(8,128)(2,1)} %bitcast.56, f32[256,1024]{1,0:T(8,128)} %copy-done.6), kind=kOutput, calls=%fused_computation.30 | convolution fusion | flops 1078722560 | bytes 6815744 | tf_op jit(solution)/shard_map/pc,pj->cj/dot_general | solution.py:614
  113.5 1.4 convolution_convert_fusion.4.cols
  114.9 1.5 convolution_convert_fusion.3
  116.4 0.1 copy-done.5
  116.5 2.7 %pad_maximum_fusion.g2 = bf16[4,2,4,2,48,768]{5,4,3,2,1,0:T(8,128)(2,1)} fusion(bf16[4,2,4,2,24,768]{5,4,3,2,1,0:T(8,128)(2,1)S(1)} %bitcast.47, bf16[4,2,4,2,24,768]{5,4,3,2,1,0:T(8,128)(2,1)S(1)} %bitcast.48), kind=kLoop, calls=%fused_computation | loop fusion | flops 9437184 | bytes 9437184 | tf_op jit(solution)/shard_map/concatenate | solution.py:613
  119.2 3.4 %convolution_convert_fusion = bf16[2048,1024]{1,0:T(8,128)(2,1)} fusion(bf16[2048,256]{1,0:T(8,128)(2,1)S(1)} %copy-done.2, f32[256,1024]{1,0:T(8,128)S(1)} %copy-done.7), kind=kOutput, calls=%fused_computation.1 | convolution fusion | flops 1078198272 | bytes 6291456 | tf_op jit(solution)/shard_map/pc,cj->pj/dot_general | solution.py:617
  122.7 1.3 convolution_convert_fusion.1
  123.9 62.1 %sums_and_to_patches.1 = (f32[16,1024]{1,0:T(8,128)S(1)}, f32[16,1024]{1,0:T(8,128)S(1)}, f32[48,768]{1,0:T(8,128)S(1)}, bf16[384,768]{1,0:T(8,128)(2,1)S(1)}) custom-call(bf16[4,2,4,2,2,16,1024]{6,5,4,3,2,1,0:T(8,128)(2,1)S(1)} %bitcast.45, bf16[4,2,4,2,2,16,1024]{6,5,4,3,2,1,0:T(8,128)(2,1)} %bitcast.46, ...), custom_call_target="tpu_custom_call" | custom-call | tf_op jit(solution)/shard_map/sums_and_to_patches/pallas_call | solution.py:566
  186.0 0.6 convert_reduce_fusion
  186.6 1.3 fusion.20
  187.9 0.7 constant_dynamic-slice_fusion
  188.5 0.6 copy.13
  189.1 0.6 copy.14
  (32 shorter events, 0.1 us)
Async XLA Ops:
  0.6 81.4 %copy-start = (bf16[1536,768]{1,0:T(8,128)(2,1)S(1)}, bf16[1536,768]{1,0:T(8,128)(2,1)}, u32[]{:S(2)}) copy-start(bf16[1536,768]{1,0:T(8,128)(2,1)} %param.10) | copy-start | bytes 7077892
  57.0 4.9 %copy-start.10 = (bf16[4,2,4,2,32,1024]{5,4,3,2,1,0:T(8,128)(2,1)S(1)}, bf16[4,2,4,2,32,1024]{5,4,3,2,1,0:T(8,128)(2,1)}, u32[]{:S(2)}) copy-start(bf16[4,2,4,2,32,1024]{5,4,3,2,1,0:T(8,128)(2,1)} %get-tuple-element.12) | copy-start | bytes 12582916
  61.0 1.0 copy-start.6
  61.9 18.4 %copy-start.1 = (bf16[6,64,768]{2,1,0:T(8,128)(2,1)S(1)}, bf16[6,64,768]{2,1,0:T(8,128)(2,1)}, u32[]{:S(2)}) copy-start(bf16[6,64,768]{2,1,0:T(8,128)(2,1)} %param.6) | copy-start | bytes 1769476
  82.0 1.2 copy-start.8
  82.0 1.9 copy-start.11
  85.9 3.1 %copy-start.12 = (bf16[384,1536]{1,0:T(8,128)(2,1)}, bf16[384,1536]{1,0:T(8,128)(2,1)S(1)}, u32[]{:S(2)}) copy-start(bf16[384,1536]{1,0:T(8,128)(2,1)S(1)} %fusion) | copy-start | bytes 3538948
  108.8 4.7 %copy-start.9 = (bf16[4,2,4,2,32,1024]{5,4,3,2,1,0:T(8,128)(2,1)S(1)}, bf16[4,2,4,2,32,1024]{5,4,3,2,1,0:T(8,128)(2,1)}, u32[]{:S(2)}) copy-start(bf16[4,2,4,2,32,1024]{5,4,3,2,1,0:T(8,128)(2,1)} %get-tuple-element.14) | copy-start | bytes 12582916
  113.5 1.4 copy-start.13
  114.9 1.7 copy-start.5
  116.5 2.7 %copy-start.2 = (bf16[2048,256]{1,0:T(8,128)(2,1)S(1)}, bf16[2048,256]{1,0:T(8,128)(2,1)}, u32[]{:S(2)}) copy-start(bf16[2048,256]{1,0:T(8,128)(2,1)} %to_channels.1) | copy-start | bytes 3145732
  116.5 2.7 %copy-start.7 = (f32[256,1024]{1,0:T(8,128)S(1)}, f32[256,1024]{1,0:T(8,128)}, u32[]{:S(2)}) copy-start(f32[256,1024]{1,0:T(8,128)} %copy-done.6) | copy-start | bytes 3145732
  119.2 3.4 %copy-start.4 = (bf16[2048,256]{1,0:T(8,128)(2,1)S(1)}, bf16[2048,256]{1,0:T(8,128)(2,1)}, u32[]{:S(2)}) copy-start(bf16[2048,256]{1,0:T(8,128)(2,1)} %get-tuple-element.13) | copy-start | bytes 3145732
  123.9 62.7 %copy-start.3 = (f32[384,768]{1,0:T(8,128)S(1)}, f32[384,768]{1,0:T(8,128)}, u32[]{:S(2)}) copy-start(f32[384,768]{1,0:T(8,128)} %get-tuple-element.24) | copy-start | bytes 3538948
